TPU v7x, 32 devices: a whole 2x2x4 slice. The times are simulated.
32 devices in a mesh: grp: 2 (over y), pb: 4 (over z), ha: 4 (over x, core).
Axes of the slice: x: 2, y: 2, z: 4, core: 2. Of those that a mesh axis runs over, the one named last changes fastest.
Arguments:
- latents: bfloat16 [8, 384, 3072], P(('grp', 'pb'), None, 'ha'), parts along dimension 0, may hold values from -6 to 6
- timesteps: int32 [8], P(('grp', 'pb')), parts along dimension 0, may hold values from 0 to 999
- mod_weight: bfloat16 [256, 3, 3072], P(None, None, 'ha'), may hold values from -0.375 to 0.375
- qkv_weight: bfloat16 [3072, 3, 3072], P(None, None, 'ha'), may hold values from -0.109375 to 0.109375
- out_weight: bfloat16 [3072, 3072], P('ha'), may hold values from -0.15625 to 0.15625
- noise_frame: bfloat16 [768, 3072], P('grp', 'ha'), parts along dimension 0, may hold values from -6 to 6
Outputs:
- advanced: bfloat16 [8, 384, 3072], P(('grp', 'pb'), None, 'ha'), parts along dimension 0
- queue_next: bfloat16 [8, 384, 3072], P(('grp', 'pb'), None, 'ha'), parts along dimension 0
There are 2 independent parts, one for each index of `grp`. A program takes and returns all parts, laid end to end along the dimension named above; an argument that names none is the same for every part. Nothing has to cross between parts.
All inputs are finite; a program needn't handle non-finite values.
Results may differ from a plain program's by a relative error of at most 0.0045.
Values may be sent and summed in bfloat16 or wider, within the bound.
A program may use at most 64 MiB of HBM per device.

v0:
```python
import math

import jax
import jax.numpy as jnp
from jax import lax
from jax.sharding import PartitionSpec as P

HD = 128
TDIM = 256


def from_behind(x, axis, by):
    size = lax.axis_size(axis)
    pairs = [(i, i + by) for i in range(size) if 0 <= i + by < size]
    return lax.ppermute(x, axis, pairs)


def sinusoid(timesteps):
    half_width = TDIM // 2
    frequency = jnp.exp(-math.log(10000.0) * jnp.arange(half_width, dtype=jnp.float32) / half_width)
    angles = timesteps.astype(jnp.float32)[:, None] * frequency[None, :]
    return jnp.concatenate([jnp.cos(angles), jnp.sin(angles)], axis=1)


def unit_rms(vectors):
    return vectors * lax.rsqrt(jnp.mean(vectors * vectors, axis=-1, keepdims=True) + 1e-06)


def absorb(running, pieces, queries, head_local):
    key_piece, value_piece = pieces

    def one_frame(position, inner):
        numerator, denominator = inner
        key_frame = lax.dynamic_index_in_dim(key_piece, position, 0, keepdims=False)
        value_frame = lax.dynamic_index_in_dim(value_piece, position, 0, keepdims=False)
        key_count = key_frame.shape[0]
        key_frame = key_frame.reshape(key_count, head_local, -1)
        value_frame = value_frame.reshape(key_count, head_local, -1)
        scores = jnp.einsum("rhd,khd->hrk", queries, key_frame, preferred_element_type=jnp.float32)
        weights_exp = jnp.exp(scores)
        denominator = denominator + jnp.sum(weights_exp, axis=2)
        numerator = numerator + jnp.einsum(
            "hrk,khd->rhd",
            weights_exp.astype(jnp.bfloat16),
            value_frame,
            preferred_element_type=jnp.float32,
        )
        return (numerator, denominator)

    return lax.fori_loop(0, key_piece.shape[0], one_frame, running)


def on_device(latents, timesteps, mod_weight, qkv_weight, out_weight, noise_frame):
    frames, tok_count, local_width = latents.shape
    full_width = qkv_weight.shape[0]
    head_size = HD
    head_local = local_width // head_size
    row_count = frames * tok_count
    out_columns = lax.all_to_all(out_weight, "ha", split_axis=1, concat_axis=0, tiled=True)
    embedding = sinusoid(timesteps).astype(jnp.bfloat16)
    modulation = jnp.dot(
        embedding,
        mod_weight.reshape(mod_weight.shape[0], 3 * local_width),
        preferred_element_type=jnp.float32,
    )
    modulation = modulation.astype(jnp.bfloat16).reshape(frames, 3, local_width)
    whole_rows, whole_mod = (
        lax.all_gather(latents, "ha", axis=2, tiled=True),
        lax.all_gather(modulation[:, :2], "ha", axis=2, tiled=True),
    )
    whole_mod = whole_mod.astype(jnp.float32)
    latent_wide = whole_rows.astype(jnp.float32)
    row_mean = jnp.mean(latent_wide, axis=-1, keepdims=True)
    centered = latent_wide - row_mean
    row_var = jnp.mean(centered * centered, axis=-1, keepdims=True)
    normed = centered * lax.rsqrt(row_var + 1e-06)
    hidden = normed * (1.0 + whole_mod[:, 1][:, None, :]) + whole_mod[:, 0][:, None, :]
    hidden = hidden.astype(jnp.bfloat16).reshape(row_count, full_width)
    projected = jnp.dot(
        hidden, qkv_weight.reshape(full_width, 3 * local_width), preferred_element_type=jnp.float32
    )
    projected = projected.reshape(row_count, 3, head_local, head_size)
    queries = (unit_rms(projected[:, 0]) / math.sqrt(head_size)).astype(jnp.bfloat16)
    key_rows = (
        unit_rms(projected[:, 1]).astype(jnp.bfloat16).reshape(frames, tok_count, local_width)
    )
    value_rows = projected[:, 2].astype(jnp.bfloat16).reshape(frames, tok_count, local_width)
    start_carry = (
        jnp.zeros((row_count, head_local, head_size), jnp.float32),
        jnp.zeros((head_local, row_count), jnp.float32),
    )
    key_all, value_all = (
        lax.all_gather(key_rows, "pb", axis=0, tiled=True),
        lax.all_gather(value_rows, "pb", axis=0, tiled=True),
    )
    numerator, denominator = absorb(start_carry, (key_all, value_all), queries, head_local)
    attended = (
        (numerator / denominator.T[:, :, None]).astype(jnp.bfloat16).reshape(row_count, local_width)
    )
    branch = jnp.dot(
        lax.all_gather(attended, "ha", axis=1, tiled=True),
        out_columns,
        preferred_element_type=jnp.float32,
    )
    branch = branch.reshape(frames, tok_count, local_width)
    gate_wide = modulation[:, 2].astype(jnp.float32)[:, None, :]
    advanced = (latents.astype(jnp.float32) + gate_wide * branch).astype(jnp.bfloat16)
    incoming = from_behind(advanced, "pb", -1)
    is_last = lax.axis_index("pb") == lax.axis_size("pb") - 1
    tail_frame = jnp.where(is_last, noise_frame[None], incoming)
    queue_next = jnp.concatenate([advanced[1:], tail_frame], axis=0)
    return (advanced, queue_next)


def solution(mesh):
    placed = (
        P(("grp", "pb"), None, "ha"),
        P(("grp", "pb")),
        P(None, None, "ha"),
        P(None, None, "ha"),
        P("ha", None),
        P("grp", "ha"),
    )
    return jax.shard_map(
        on_device,
        mesh=mesh,
        in_specs=placed,
        out_specs=(P(("grp", "pb"), None, "ha"), P(("grp", "pb"), None, "ha")),
        check_vma=False,
    )
```

profile of v0, /device:TPU:0, one launch (start us, length us, event | category | flops | bytes accessed | tf_op | source)
XLA Modules:
  0.0 259.0 jit_solution(10674421774756293584)
XLA Ops:
  7.2 0.0 all-gather.5.cloned.1.call-start
  7.2 0.7 all-gather.5.cloned.1.call-update
  7.9 0.0 all-gather.9.cloned.1.call-start
  8.6 0.1 sine_convert_fusion
  8.7 1.6 copy.26
  10.2 0.5 convolution_reduce_fusion
  10.8 0.6 copy-done.4
  11.3 6.1 %all_gather.16 = bf16[1,2,3072]{2,1,0:T(2,128)(2,1)S(1)} all-gather(bf16[1,2,768]{2,1,0:T(2,128)(2,1)S(1)} %slice.30), channel_id=1, replica_groups=mesh['grp'=2,'pb'=4,'ha'=4] {'ha'}, dimensions={2}, use_global_device_ids=true | all-gather | bytes 15360 | tf_op jit(solution)/shard_map/all_gather | solution.py:69
  17.5 17.4 %copy.27 = bf16[3072,3,768]{0,2,1:T(8,128)(2,1)} copy(bf16[3072,3,768]{2,0,1:T(8,128)(2,1)} %param.11) | data formatting | bytes 28311552 | tf_op args[3]
  34.9 0.6 slice_add_fusion
  35.5 0.8 all-gather.5.cloned.1.call-done
  36.4 2.2 convert_reduce_fusion
  38.6 0.2 copy-done
  38.7 0.8 fusion.5
  39.5 10.7 %fusion.10 = f32[384,3,6,128]{0,3,2,1:T(8,128)S(1)} fusion(bf16[3,6,128,3072]{3,2,1,0:T(8,128)(2,1)} %bitcast.84, bf16[1,384,3072]{2,1,0:T(8,128)(2,1)S(1)} %copy-done, f32[3072]{0:T(1024)S(1)} %bitcast.88, f32[3072]{0:T(1024)S(1)} %bitcast.89, f32[384]{0:T(512)S(1)} %add_rsqrt_fusion.2, f32[384]{0:T(512)S(1)} %broadcast_multiply_fusion), kind=kOutput, calls=%fused_computation.17 | convolution fusion | flops 5442895872 | bytes 20081664 | tf_op jit(solution)/shard_map/dot_general | solution.py:79
  50.2 0.1 multiply_reduce_fusion.1
  50.4 0.9 fusion.19
  51.3 2.1 copy.29
  53.4 0.0 all-gather.9.cloned.1.call-update
  53.5 0.0 all-gather.7.cloned.1.call-start
  53.5 0.9 slice.47
  54.4 2.1 copy.28
  56.5 0.0 all-gather.7.cloned.1.call-update
  56.5 6.7 %copy.33 = bf16[768,3072]{0,1:T(8,128)(2,1)} copy(bf16[768,3072]{1,0:T(8,128)(2,1)} %param.12) | data formatting | bytes 9437184 | tf_op args[4]
  63.3 4.9 %all-to-all-start = ((bf16[768,4,768]{0,2,1:T(8,128)(2,1)}), bf16[768,4,768]{0,2,1:T(8,128)(2,1)}, u32[]{:S(2)}, u32[]{:S(2)}) async-start(bf16[768,4,768]{0,2,1:T(8,128)(2,1)} %bitcast.83), calls=%async_computation | async-start | bytes 9437184 | tf_op jit(solution)/shard_map/all_to_all | solution.py:59
  68.2 0.0 all-gather.11.cloned.1.call-start
  68.3 0.1 multiply_reduce_fusion
  68.4 0.9 multiply_convert_fusion
  69.3 2.2 copy.32
  71.5 34.8 %all-gather.9.cloned.1.call-done = bf16[4,384,768]{2,1,0:T(8,128)(2,1)} async-done(((bf16[1,384,768]{2,1,0:T(8,128)(2,1)}), bf16[4,384,768]{2,1,0:T(8,128)(2,1)}) %all-gather.9.cloned.1.call-update) | async-done | bytes 2359312 | tf_op jit(solution)/shard_map/all_gather | solution.py:93
  106.3 51.5 %all-gather.7.cloned.1.call-done = bf16[4,384,768]{2,1,0:T(8,128)(2,1)} async-done(((bf16[1,384,768]{2,1,0:T(8,128)(2,1)}), bf16[4,384,768]{2,1,0:T(8,128)(2,1)}) %all-gather.7.cloned.1.call-update) | async-done | bytes 2359312 | tf_op jit(solution)/shard_map/all_gather | solution.py:94
  157.8 45.9 %while.16 = (s32[]{:T(128)}, f32[384,6,128]{0,2,1:T(8,128)}, f32[6,384]{1,0:T(8,128)}, bf16[4,384,768]{2,1,0:T(8,128)(2,1)}, bf16[4,384,768]{2,1,0:T(8,128)(2,1)...) while((s32[]{:T(128)}, f32[384,6,128]{0,2,1:T(8,128)}, f32[6,384]{1,0:T(8,128)}, ...), condition=%wide.region_6.7_spmd.clone, body=%wide.region_4.6_spmd.clone.sunk | while | flops 455346432 | bytes 15962212 | solution.py:50
  157.8 2.1 constant_dynamic-slice_fusion.3
  159.9 1.1 copy.43
  161.0 2.0 bitcast_reduce_fusion.2
  163.0 2.1 copy.42
  165.1 2.8 %fusion.36 = f32[384,6,128]{0,2,1:T(8,128)} fusion(bf16[384,6,128]{0,2,1:T(8,128)(2,1)} %bitcast.80, f32[6,384,384]{2,1,0:T(8,128)S(1)} %get-tuple-element.222, f32[384,6,128]{0,2,1:T(8,128)} %get-tuple-element.233, pred[]{:T(512)S(6)} %compare.3), kind=kOutput, calls=%fused_computation.4.clone.1 | convolution fusion | flops 227966976 | bytes 6488065 | tf_op jit(solution)/shard_map/while/body/eval_jaxpr/hrk,khd->rhd/dot_general | solution.py:42
  167.9 0.6 select_add_fusion.2
  168.5 2.1 constant_dynamic-slice_fusion.3
  170.6 1.1 copy.43
  171.7 2.0 bitcast_reduce_fusion.2
  173.7 2.1 copy.42
  175.8 3.1 %fusion.36 = f32[384,6,128]{0,2,1:T(8,128)} fusion(bf16[384,6,128]{0,2,1:T(8,128)(2,1)} %bitcast.80, f32[6,384,384]{2,1,0:T(8,128)S(1)} %get-tuple-element.222, f32[384,6,128]{0,2,1:T(8,128)} %get-tuple-element.233, pred[]{:T(512)S(6)} %compare.3), kind=kOutput, calls=%fused_computation.4.clone.1 | convolution fusion | flops 227966976 | bytes 6488065 | tf_op jit(solution)/shard_map/while/body/eval_jaxpr/hrk,khd->rhd/dot_general | solution.py:42
  178.9 1.3 select_add_fusion.2
  180.2 2.1 constant_dynamic-slice_fusion.3
  182.4 1.1 copy.43
  183.4 2.0 bitcast_reduce_fusion.2
  185.4 2.1 copy.42
  187.5 3.1 %fusion.36 = f32[384,6,128]{0,2,1:T(8,128)} fusion(bf16[384,6,128]{0,2,1:T(8,128)(2,1)} %bitcast.80, f32[6,384,384]{2,1,0:T(8,128)S(1)} %get-tuple-element.222, f32[384,6,128]{0,2,1:T(8,128)} %get-tuple-element.233, pred[]{:T(512)S(6)} %compare.3), kind=kOutput, calls=%fused_computation.4.clone.1 | convolution fusion | flops 227966976 | bytes 6488065 | tf_op jit(solution)/shard_map/while/body/eval_jaxpr/hrk,khd->rhd/dot_general | solution.py:42
  190.7 1.3 select_add_fusion.2
  192.0 2.1 constant_dynamic-slice_fusion.3
  194.1 1.1 copy.43
  195.2 2.0 bitcast_reduce_fusion.2
  197.2 2.1 copy.42
  199.3 3.1 %fusion.36 = f32[384,6,128]{0,2,1:T(8,128)} fusion(bf16[384,6,128]{0,2,1:T(8,128)(2,1)} %bitcast.80, f32[6,384,384]{2,1,0:T(8,128)S(1)} %get-tuple-element.222, f32[384,6,128]{0,2,1:T(8,128)} %get-tuple-element.233, pred[]{:T(512)S(6)} %compare.3), kind=kOutput, calls=%fused_computation.4.clone.1 | convolution fusion | flops 227966976 | bytes 6488065 | tf_op jit(solution)/shard_map/while/body/eval_jaxpr/hrk,khd->rhd/dot_general | solution.py:42
  202.4 1.3 select_add_fusion.2
  203.8 2.2 divide_convert_fusion
  205.9 0.0 all-gather.11.cloned.1.call-update
  206.0 6.8 %copy.34 = bf16[4,768,768]{2,1,0:T(8,128)(2,1)} copy(bf16[4,768,768]{1,2,0:T(8,128)(2,1)} %bitcast.17) | data formatting | bytes 9437184 | tf_op jit(solution)/shard_map/all_to_all | solution.py:59
  212.8 16.2 %all-gather.11.cloned.1.call-done = bf16[384,3072]{0,1:T(8,128)(2,1)} async-done(((bf16[384,768]{0,1:T(8,128)(2,1)}), bf16[384,3072]{0,1:T(8,128)(2,1)}) %all-gather.11.cloned.1.call-update) | async-done | bytes 2359312 | tf_op jit(solution)/shard_map/all_gather | solution.py:101
  229.0 5.1 %fusion.18 = bf16[1,384,768]{2,1,0:T(8,128)(2,1)S(1)} fusion(bf16[384,3072]{0,1:T(8,128)(2,1)} %all-gather.11.cloned.1.call-done, bf16[3072,768]{1,0:T(8,128)(2,1)} %bitcast.82, bf16[1,384,768]{2,1,0:T(8,128)(2,1)S(1)} %copy-done.1, f32[768]{0:T(1024)S(1)} %fusion.20), kind=kOutput, calls=%fused_computation.25 | convolution fusion | flops 1813118976 | bytes 8260608 | tf_op jit(solution)/shard_map/dot_general | solution.py:100
  234.2 1.3 collective-permute-start
  235.5 16.1 %collective-permute-done = bf16[1,384,768]{2,1,0:T(8,128)(2,1)S(1)} collective-permute-done((bf16[1,384,768]{2,1,0:T(8,128)(2,1)S(1)}, bf16[1,384,768]{2,1,0:T(8,128)(2,1)S(1)}, u32[]{:S(2)}, u32[]{:S(2)}) %collective-permute-start) | collective-permute-done | bytes 589856 | tf_op jit(solution)/shard_map/ppermute | solution.py:15
  251.5 0.9 bitcast_select_fusion
  (26 shorter events, 0.1 us)
Async XLA Ops:
  7.2 29.2 %all-gather.5.cloned.1.call-start = ((), (), s32[]{:S(2)}) async-start(), calls=%async_computation.1 | async-start | bytes 2949120 | tf_op jit(solution)/shard_map/all_gather | solution.py:68
  7.9 98.4 %all-gather.9.cloned.1.call-start = ((), (), s32[]{:S(2)}) async-start(), calls=%async_computation.3 | async-start | bytes 2949120 | tf_op jit(solution)/shard_map/all_gather | solution.py:93
  10.7 0.6 copy-start.4
  36.4 2.4 copy-start
  36.4 3.1 %copy-start.6 = (f32[1,1,3072]{2,1,0:T(1,128)S(1)}, f32[1,1,3072]{2,1,0:T(1,128)}, u32[]{:S(2)}) copy-start(f32[1,1,3072]{2,1,0:T(1,128)} %slice_add_fusion) | copy-start | bytes 36868
  53.5 104.3 %all-gather.7.cloned.1.call-start = ((), (), s32[]{:S(2)}) async-start(), calls=%async_computation.2 | async-start | bytes 2949120 | tf_op jit(solution)/shard_map/all_gather | solution.py:94
  63.3 142.8 %all-to-all-start = ((bf16[768,4,768]{0,2,1:T(8,128)(2,1)}), bf16[768,4,768]{0,2,1:T(8,128)(2,1)}, u32[]{:S(2)}, u32[]{:S(2)}) async-start(bf16[768,4,768]{0,2,1:T(8,128)(2,1)} %bitcast.83), calls=%async_computation | async-start | bytes 9437184 | tf_op jit(solution)/shard_map/all_to_all | solution.py:59
  68.2 160.8 %all-gather.11.cloned.1.call-start = ((), (), s32[]{:S(2)}) async-start(), calls=%async_computation.4 | async-start | bytes 2949120 | tf_op jit(solution)/shard_map/all_gather | solution.py:101
  203.7 2.2 copy-start.5
  206.0 23.0 %copy-start.1 = (bf16[1,384,768]{2,1,0:T(8,128)(2,1)S(1)}, bf16[1,384,768]{2,1,0:T(8,128)(2,1)}, u32[]{:S(2)}) copy-start(bf16[1,384,768]{2,1,0:T(8,128)(2,1)} %param.8) | copy-start | bytes 1769476
  229.0 22.5 %copy-start.3 = (bf16[384,768]{1,0:T(8,128)(2,1)S(1)}, bf16[384,768]{1,0:T(8,128)(2,1)}, u32[]{:S(2)}) copy-start(bf16[384,768]{1,0:T(8,128)(2,1)} %param.13) | copy-start | bytes 1769476
  234.2 18.3 %copy-start.2 = (bf16[1,384,768]{2,1,0:T(8,128)(2,1)}, bf16[1,384,768]{2,1,0:T(8,128)(2,1)S(1)}, u32[]{:S(2)}) copy-start(bf16[1,384,768]{2,1,0:T(8,128)(2,1)S(1)} %fusion.18) | copy-start | bytes 1769476
  234.2 17.4 %collective-permute-start = (bf16[1,384,768]{2,1,0:T(8,128)(2,1)S(1)}, bf16[1,384,768]{2,1,0:T(8,128)(2,1)S(1)}, u32[]{:S(2)}, u32[]{:S(2)}) collective-permute-start(bf16[1,384,768]{2,1,0:T(8,128)(2,1)S(1)} %fusion.18), channel_id=1, source_target_pairs={{4,0},{8,4},{12,8},{5,1},{9,5},{13,9},{6,2},{10,6},{14,10},{7,3},{... | collective-permute-start | bytes 1769480 | tf_op jit(solution)/shard_map/ppermute | solution.py:15
Sparse Core Ops, SparseCore 0:
  9.6 26.7 all-gather.4
  53.6 52.6 all-gather.8
  108.5 49.2 all-gather.6
  206.1 22.8 all-gather.10
where the time goes:
time: 261 us; the launch traced here: 259 us
  waiting for transfers between devices  120 us (46%)
  local copies, waits for them, and re-layouts  61.8 us (24%)
  matrix products  36.4 us (14%)
  between operations  14.6 us (6%)
  other arithmetic  13.4 us (5%)
  starting transfers between devices  6.4 us (2%)
  blocking collectives  6.14 us (2%)
    all_gather x1, waiting for transfers between devices, on_device(): lax.all_gather(value_rows, 'pb', axis=0, tiled=True)  51.5 us
    all_gather x1, waiting for transfers between devices, on_device(): lax.all_gather(key_rows, 'pb', axis=0, tiled=True)  34.8 us
    unnamed x18, local copies, waits for them, and re-layouts  28.6 us
    all_gather x1, waiting for transfers between devices, on_device(): lax.all_gather(attended, 'ha', axis=1, tiled=True)  16.2 us
    ppermute x1, waiting for transfers between devices, from_behind(): return lax.ppermute(x, axis, pairs)  16.1 us
    dynamic_slice x8, local copies, waits for them, and re-layouts, one_frame(): key_frame = lax.dynamic_index_in_dim(key_piece, position, 0, keepdims=False)  12.7 us
    dot_general x4, matrix products, one_frame(): jnp.einsum('hrk,khd->rhd', weights_exp.astype(jnp.bfloat16), value_frame,...  12.2 us
    dot_general x1, matrix products, on_device(): jnp.dot(hidden, qkv_weight.reshape(full_width, 3 * local_width), preferre...  10.7 us
  transfers between devices with their start and end apart: 6, of which 5 were waited for; matrix products, arithmetic and copies ran while one was open for 34% of the time, Pallas kernels for 0%

commit v1 on v0

--- a/solution.py
+++ b/solution.py
@@ -1,8 +1,11 @@
+import functools
 import math
 
 import jax
 import jax.numpy as jnp
 from jax import lax
+from jax.experimental import pallas as pl
+from jax.experimental.pallas import tpu as pltpu
 from jax.sharding import PartitionSpec as P
 
 HD = 128
@@ -112,6 +115,473 @@
     return (advanced, queue_next)
 
 
+EXTRA = 16
+LN_ROWS = 16
+CHUNKS = 4
+MESH = pl.DeviceIdType.MESH
+F32 = jnp.float32
+BF16 = jnp.bfloat16
+
+
+def pick(table, index):
+    value = jnp.int32(table[0])
+    for i in range(1, len(table)):
+        value = jnp.where(index == i, jnp.int32(table[i]), value)
+    return value
+
+
+def frame_order(size):
+    orders = []
+    for z in range(size):
+        order = [z]
+        for d in range(1, size):
+            order += [f for f in (z + d, z - d) if 0 <= f < size]
+        orders.append(order)
+    return orders
+
+
+def block_kernel(
+    size,
+    emb_ref,
+    lat_hbm,
+    modw_hbm,
+    w_hbm,
+    wo_hbm,
+    noise_hbm,
+    adv_hbm,
+    next_hbm,
+    lat,
+    modw,
+    w,
+    wo,
+    hid,
+    mods,
+    gate,
+    qbuf,
+    num,
+    den,
+    own,
+    xpart,
+    sbuf,
+    rbuf,
+    xbuf,
+    xrecv,
+    adv,
+    nxt,
+    load_sem,
+    left_sem,
+    right_sem,
+    xs_sem,
+    ss_sem,
+    zr_sem,
+    xr_sem,
+    sr_sem,
+    tail_ss,
+    tail_sr,
+    tail_xs,
+    tail_xr,
+    tail_zs,
+    tail_zr,
+    adv_sem,
+    nxt_sem,
+):
+    z = lax.axis_index("pb")
+    h = lax.axis_index("ha")
+    core = lax.rem(h, 2)
+    sib = h + 1 - 2 * core
+    xp = lax.rem(h + 2, 4)
+    far = 3 - h
+    tok = lat_hbm.shape[1]
+    wid = lat_hbm.shape[2]
+    full = 4 * wid
+    pairs = wid // (2 * HD)
+    rows = tok // CHUNKS
+    has_left = z > 0
+    has_right = z < size - 1
+
+    load_lat = pltpu.make_async_copy(
+        lat_hbm.at[0], lat.at[z, h, pl.ds(0, tok)], load_sem.at[0]
+    )
+    load_modw = pltpu.make_async_copy(modw_hbm, modw, load_sem.at[1])
+    load_w = pltpu.make_async_copy(w_hbm, w, load_sem.at[2])
+    load_wo = pltpu.make_async_copy(wo_hbm, wo, load_sem.at[3])
+    move_noise = pltpu.make_async_copy(noise_hbm, next_hbm.at[0], load_sem.at[4])
+    load_modw.start()
+    load_lat.start()
+
+    barrier = pltpu.get_barrier_semaphore()
+    pl.semaphore_signal(barrier, inc=1, device_id={"ha": sib}, device_id_type=MESH)
+    pl.semaphore_signal(barrier, inc=1, device_id={"ha": xp}, device_id_type=MESH)
+
+    @pl.when(has_left)
+    def _():
+        pl.semaphore_signal(barrier, inc=1, device_id={"pb": z - 1}, device_id_type=MESH)
+
+    @pl.when(has_right)
+    def _():
+        pl.semaphore_signal(barrier, inc=1, device_id={"pb": z + 1}, device_id_type=MESH)
+
+    load_modw.wait()
+    gate_row = None
+    lines = []
+    for j in range(3):
+        made = jnp.dot(emb_ref[...], modw[j], preferred_element_type=F32).astype(BF16)
+        lines.append(made.astype(F32))
+    gate[...] = lines[2][0:8]
+    row_id = lax.broadcasted_iota(jnp.int32, (EXTRA, wid), 0)
+    lat[z, h, pl.ds(tok, EXTRA), :] = jnp.where(row_id == 0, lines[0], lines[1]).astype(BF16)
+    load_lat.wait()
+
+    waits = 2 + has_left.astype(jnp.int32) + has_right.astype(jnp.int32)
+    pl.semaphore_wait(barrier, waits)
+
+    def to_left(f):
+        return pltpu.make_async_remote_copy(
+            lat.at[f, h], lat.at[f, h], left_sem.at[f], zr_sem.at[f], {"pb": z - 1}, MESH
+        )
+
+    def to_right(f):
+        return pltpu.make_async_remote_copy(
+            lat.at[f, h], lat.at[f, h], right_sem.at[f], zr_sem.at[f], {"pb": z + 1}, MESH
+        )
+
+    def to_x(f):
+        return pltpu.make_async_remote_copy(
+            lat.at[f, h], lat.at[f, h], xs_sem.at[f], xr_sem.at[f], {"ha": xp}, MESH
+        )
+
+    def from_x(f):
+        return pltpu.make_async_remote_copy(
+            lat.at[f, h], lat.at[f, xp], xs_sem.at[f], xr_sem.at[f], {"ha": xp}, MESH
+        )
+
+    def to_sib(f, which):
+        quarter = h if which == 0 else xp
+        return pltpu.make_async_remote_copy(
+            lat.at[f, quarter],
+            lat.at[f, quarter],
+            ss_sem.at[which, f],
+            sr_sem.at[which, f],
+            {"ha": sib},
+            MESH,
+        )
+
+    def from_sib(f, which):
+        quarter = sib if which == 0 else far
+        return pltpu.make_async_remote_copy(
+            lat.at[f, quarter],
+            lat.at[f, quarter],
+            ss_sem.at[which, f],
+            sr_sem.at[which, f],
+            {"ha": sib},
+            MESH,
+        )
+
+    @pl.when(has_left)
+    def _():
+        to_left(z).start()
+
+    @pl.when(has_right)
+    def _():
+        to_right(z).start()
+
+    to_x(z).start()
+    to_sib(z, 0).start()
+    load_w.start()
+    load_wo.start()
+
+    @pl.when(z == size - 1)
+    def _():
+        move_noise.start()
+
+    num[...] = jnp.zeros_like(num)
+    den[...] = jnp.zeros_like(den)
+
+    orders = frame_order(size)
+    load_w.wait()
+
+    def step(s, carry):
+        d = s + 1
+
+        @pl.when(z + d < size)
+        def _():
+            f = z + d
+            to_right(f).wait_recv()
+
+            @pl.when(has_left)
+            def _():
+                to_left(f).start()
+
+            to_x(f).start()
+            to_sib(f, 0).start()
+
+        @pl.when(z - d >= 0)
+        def _():
+            f = z - d
+            to_left(f).wait_recv()
+
+            @pl.when(has_right)
+            def _():
+                to_right(f).start()
+
+            to_x(f).start()
+            to_sib(f, 0).start()
+
+        f = jnp.int32(0)
+        for i in range(size):
+            f = jnp.where(s == i, pick([o[i] for o in orders], z), f)
+        from_x(f).wait_recv()
+        to_sib(f, 1).start()
+        from_sib(f, 0).wait_recv()
+        from_sib(f, 1).wait_recv()
+
+        for q in range(4):
+            extra = lat[f, q, pl.ds(tok, EXTRA), :].astype(F32)
+            mods[0, :, q * wid : (q + 1) * wid] = jnp.broadcast_to(extra[0:1], (8, wid))
+            mods[1, :, q * wid : (q + 1) * wid] = jnp.broadcast_to(1.0 + extra[1:2], (8, wid))
+
+        def norm_rows(t, inner):
+            r = pl.ds(pl.multiple_of(t * LN_ROWS, LN_ROWS), LN_ROWS)
+            parts = [lat[f, q, r, :].astype(F32) for q in range(4)]
+            total = parts[0] + parts[1] + parts[2] + parts[3]
+            mean = jnp.sum(total, axis=-1, keepdims=True) * (1.0 / full)
+            parts = [part - mean for part in parts]
+            squares = parts[0] * parts[0]
+            for part in parts[1:]:
+                squares = squares + part * part
+            var = jnp.sum(squares, axis=-1, keepdims=True) * (1.0 / full)
+            scale = lax.rsqrt(var + 1e-06)
+            for q in range(4):
+                cols = slice(q * wid, (q + 1) * wid)
+                out = parts[q] * scale * mods[1, 0:1, cols] + mods[0, 0:1, cols]
+                hid[r, cols] = out.astype(BF16)
+            return inner
+
+        lax.fori_loop(0, tok // LN_ROWS, norm_rows, 0)
+
+        def one_pair(p, inner):
+            cols = pl.ds(pl.multiple_of(p * 2 * HD, 2 * HD), 2 * HD)
+
+            @pl.when(s == 0)
+            def _():
+                q2 = jnp.dot(hid[...], w[0, :, cols], preferred_element_type=F32)
+                halves = [
+                    unit_rms(q2[:, i * HD : (i + 1) * HD]) / math.sqrt(HD) for i in range(2)
+                ]
+                qbuf[:, cols] = jnp.concatenate(halves, axis=1).astype(BF16)
+
+            k2 = jnp.dot(hid[...], w[1, :, cols], preferred_element_type=F32)
+            keys = [unit_rms(k2[:, i * HD : (i + 1) * HD]).astype(BF16) for i in range(2)]
+            values = jnp.dot(hid[...], w[2, :, cols], preferred_element_type=F32).astype(BF16)
+            for i in range(2):
+                head = pl.ds(pl.multiple_of(p * 2 * HD + i * HD, HD), HD)
+                scores = lax.dot_general(
+                    qbuf[:, head], keys[i], (((1,), (1,)), ((), ())), preferred_element_type=F32
+                )
+                weights = jnp.exp(scores)
+                den[:, head] += jnp.broadcast_to(
+                    jnp.sum(weights, axis=1, keepdims=True), (tok, HD)
+                )
+                num[:, head] += jnp.dot(
+                    weights.astype(BF16),
+                    values[:, i * HD : (i + 1) * HD],
+                    preferred_element_type=F32,
+                )
+            return inner
+
+        lax.fori_loop(0, pairs, one_pair, 0)
+        return carry
+
+    lax.fori_loop(0, size, step, 0)
+    load_wo.wait()
+
+    def chunk(r):
+        return pl.ds(pl.multiple_of(r * rows, rows), rows)
+
+    def sib_copy(r):
+        return pltpu.make_async_remote_copy(
+            sbuf.at[r], rbuf.at[r], tail_ss.at[r], tail_sr.at[r], {"ha": sib}, MESH
+        )
+
+    def x_copy(r):
+        return pltpu.make_async_remote_copy(
+            xbuf.at[r], xrecv.at[r], tail_xs.at[r], tail_xr.at[r], {"ha": xp}, MESH
+        )
+
+    def z_send(r):
+        return pltpu.make_async_remote_copy(
+            adv.at[r], nxt.at[r], tail_zs.at[r], tail_zr.at[r], {"pb": z - 1}, MESH
+        )
+
+    def z_recv(r):
+        return pltpu.make_async_remote_copy(
+            adv.at[r], nxt.at[r], tail_zs.at[r], tail_zr.at[r], {"pb": z + 1}, MESH
+        )
+
+    def adv_out(r):
+        return pltpu.make_async_copy(adv.at[r], adv_hbm.at[0, chunk(r)], adv_sem.at[r])
+
+    def nxt_out(r):
+        return pltpu.make_async_copy(nxt.at[r], next_hbm.at[0, chunk(r)], nxt_sem.at[r])
+
+    def project(att, quarter):
+        cols = pl.ds(pl.multiple_of(quarter * wid, wid), wid)
+        return jnp.dot(att, wo[:, cols], preferred_element_type=F32)
+
+    def partials(t, carry):
+        @pl.when(t < CHUNKS)
+        def _():
+            att = (num[chunk(t), :] / den[chunk(t), :]).astype(BF16)
+            sbuf[t, 1] = project(att, far).astype(BF16)
+            sbuf[t, 0] = project(att, sib).astype(BF16)
+            sib_copy(t).start()
+            xpart[t] = project(att, xp)
+            own[t] = project(att, h)
+
+        @pl.when(t >= 1)
+        def _():
+            r = t - 1
+            sib_copy(r).wait_recv()
+            xbuf[r] = (xpart[r] + rbuf[r, 1].astype(F32)).astype(BF16)
+            x_copy(r).start()
+
+        return carry
+
+    lax.fori_loop(0, CHUNKS + 1, partials, 0)
+
+    def finish(r, carry):
+        x_copy(r).wait_recv()
+        branch = own[r] + rbuf[r, 0].astype(F32) + xrecv[r].astype(F32)
+        latent = lat[z, h, chunk(r), :].astype(F32)
+        adv[r] = (latent + gate[0:1] * branch).astype(BF16)
+
+        @pl.when(has_left)
+        def _():
+            z_send(r).start()
+
+        adv_out(r).start()
+        return carry
+
+    lax.fori_loop(0, CHUNKS, finish, 0)
+
+    def drain_frames(f, carry):
+        to_x(f).wait_send()
+        to_sib(f, 0).wait_send()
+        to_sib(f, 1).wait_send()
+
+        @pl.when(has_left & (f >= z))
+        def _():
+            to_left(f).wait_send()
+
+        @pl.when(has_right & (f <= z))
+        def _():
+            to_right(f).wait_send()
+
+        return carry
+
+    lax.fori_loop(0, size, drain_frames, 0)
+
+    def take_next(r, carry):
+        @pl.when(has_right)
+        def _():
+            z_recv(r).wait_recv()
+            nxt_out(r).start()
+
+        return carry
+
+    lax.fori_loop(0, CHUNKS, take_next, 0)
+
+    def drain_tail(r, carry):
+        sib_copy(r).wait_send()
+        x_copy(r).wait_send()
+        adv_out(r).wait()
+
+        @pl.when(has_left)
+        def _():
+            z_send(r).wait_send()
+
+        @pl.when(has_right)
+        def _():
+            nxt_out(r).wait()
+
+        return carry
+
+    lax.fori_loop(0, CHUNKS, drain_tail, 0)
+
+    @pl.when(z == size - 1)
+    def _():
+        move_noise.wait()
+
+
+def fused(size, latents, timesteps, mod_weight, qkv_weight, out_weight, noise_frame):
+    _, tok, wid = latents.shape
+    full = 4 * wid
+    rows = tok // CHUNKS
+    embedding = sinusoid(timesteps).astype(BF16)
+    embedding = jnp.broadcast_to(embedding, (EXTRA, TDIM))
+    anywhere = pl.BlockSpec(memory_space=pl.ANY)
+    dma = pltpu.SemaphoreType.DMA
+    flops = 2 * tok * full * wid * (1 + 2 * size) + 4 * tok * tok * size * wid + 2 * tok * wid * full
+    return pl.pallas_call(
+        functools.partial(block_kernel, size),
+        out_shape=(
+            jax.ShapeDtypeStruct(latents.shape, BF16),
+            jax.ShapeDtypeStruct(latents.shape, BF16),
+        ),
+        in_specs=[pl.BlockSpec(memory_space=pltpu.VMEM)] + [anywhere] * 5,
+        out_specs=(anywhere, anywhere),
+        scratch_shapes=[
+            pltpu.VMEM((size, 4, tok + EXTRA, wid), BF16),
+            pltpu.VMEM((3, TDIM, wid), BF16),
+            pltpu.VMEM((3, full, wid), BF16),
+            pltpu.VMEM((wid, full), BF16),
+            pltpu.VMEM((tok, full), BF16),
+            pltpu.VMEM((2, 8, full), F32),
+            pltpu.VMEM((8, wid), F32),
+            pltpu.VMEM((tok, wid), BF16),
+            pltpu.VMEM((tok, wid), F32),
+            pltpu.VMEM((tok, wid), F32),
+            pltpu.VMEM((CHUNKS, rows, wid), F32),
+            pltpu.VMEM((CHUNKS, rows, wid), F32),
+            pltpu.VMEM((CHUNKS, 2, rows, wid), BF16),
+            pltpu.VMEM((CHUNKS, 2, rows, wid), BF16),
+            pltpu.VMEM((CHUNKS, rows, wid), BF16),
+            pltpu.VMEM((CHUNKS, rows, wid), BF16),
+            pltpu.VMEM((CHUNKS, rows, wid), BF16),
+            pltpu.VMEM((CHUNKS, rows, wid), BF16),
+            dma((5,)),
+            dma((size,)),
+            dma((size,)),
+            dma((size,)),
+            dma((2, size)),
+            dma((size,)),
+            dma((size,)),
+            dma((2, size)),
+            dma((CHUNKS,)),
+            dma((CHUNKS,)),
+            dma((CHUNKS,)),
+            dma((CHUNKS,)),
+            dma((CHUNKS,)),
+            dma((CHUNKS,)),
+            dma((CHUNKS,)),
+            dma((CHUNKS,)),
+        ],
+        compiler_params=pltpu.CompilerParams(
+            collective_id=0, has_side_effects=True, vmem_limit_bytes=58 * 1024 * 1024
+        ),
+        cost_estimate=pl.CostEstimate(
+            flops=flops, bytes_accessed=22_000_000, transcendentals=tok * tok * size * wid // HD
+        ),
+    )(
+        embedding,
+        latents,
+        mod_weight.transpose(1, 0, 2),
+        qkv_weight.transpose(1, 0, 2),
+        out_weight,
+        noise_frame,
+    )
+
+
 def solution(mesh):
     placed = (
         P(("grp", "pb"), None, "ha"),
@@ -121,8 +591,9 @@
         P("ha", None),
         P("grp", "ha"),
     )
+    small = mesh.shape["ha"] == 4 and mesh.shape["pb"] <= 4
     return jax.shard_map(
-        on_device,
+        functools.partial(fused, mesh.shape["pb"]) if small else on_device,
         mesh=mesh,
         in_specs=placed,
         out_specs=(P(("grp", "pb"), None, "ha"), P(("grp", "pb"), None, "ha")),

time: 261 us -> 108 us (0.41)
  waiting for transfers between devices: 120 us -> 0 us
  Pallas kernels: 0 us -> 101 us
  local copies, waits for them, and re-layouts: 61.8 us -> 4.44 us
  matrix products: 36.4 us -> 0 us
  other arithmetic: 13.4 us -> 0.06 us
  between operations: 14.6 us -> 1.3 us
  starting transfers between devices: 6.4 us -> 0 us
  blocking collectives: 6.14 us -> 0 us
    all_gather x4 -> x0, waiting for transfers between devices: 103 us -> none  [the longest x1 51.5 us: on_device(): lax.all_gather(value_rows, 'pb', axis=0, tiled=True)]
    pallas_call x0 -> x1, Pallas kernels: none -> 101 us  [fused(): pl.pallas_call(functools.partial(block_kernel, size), out_shape=(jax.Shap...]
    dot_general x11 -> x0, matrix products: 36.4 us -> none  [the longest x4 12.2 us: one_frame(): jnp.einsum('hrk,khd->rhd', weights_exp.astype(jnp.bfloat16), value_frame,...]
    unnamed x18 -> x2, local copies, waits for them, and re-layouts: 28.6 us -> 3.83 us
    dynamic_slice x12 -> x0, local copies, waits for them, and re-layouts: 21.2 us -> none  [the longest x8 12.7 us: one_frame(): key_frame = lax.dynamic_index_in_dim(key_piece, position, 0, keepdims=False)]
    ppermute x1 -> x0, waiting for transfers between devices: 16.1 us -> none  [from_behind(): return lax.ppermute(x, axis, pairs)]
    all_to_all x1 -> x0, local copies, waits for them, and re-layouts: 6.79 us -> none  [on_device(): lax.all_to_all(out_weight, 'ha', split_axis=1, concat_axis=0, tiled=True)]
    all_gather x1 -> x0, blocking collectives: 6.14 us -> none  [on_device(): lax.all_gather(modulation[:, :2], 'ha', axis=2, tiled=True)]
  transfers between devices with their start and end apart: 6 -> 0, of which waited for: 5 -> 0; matrix products, arithmetic and copies ran while one was open for 34% -> 0% of each run, Pallas kernels for 0% -> 0%
where the time goes in v1:
time: 108 us; the launch traced here: 107 us
  Pallas kernels  101 us (94%)
  local copies, waits for them, and re-layouts  4.44 us (4%)
  between operations  1.3 us (1%)
    pallas_call x1, Pallas kernels, fused(): pl.pallas_call(functools.partial(block_kernel, size), out_shape=(jax.Shap...  101 us
    unnamed x2, local copies, waits for them, and re-layouts  3.83 us

profile of v1, /device:TPU:0, one launch (start us, length us, event | category | flops | bytes accessed | tf_op | source)
XLA Modules:
  0.0 107.1 jit_solution(16413807864217727267)
XLA Ops:
  1.3 0.1 sine_convert_fusion
  1.3 0.6 broadcast_in_dim.2.emb_ref
  2.0 101.3 %shard_map.77 = (bf16[1,384,768]{2,1,0:T(8,128)(2,1)}, bf16[1,384,768]{2,1,0:T(8,128)(2,1)}) custom-call(bf16[16,256]{1,0:T(8,128)(2,1)} %broadcast_in_dim.2.emb_ref, bf16[1,384,768]{2,1,0:T(8,128)(2,1)} %lat_hbm.1, bf16[3,256,768]{2,1,0:T(8,128)(2,1)} %bitcast.4, bf16[3,3072,768]{2,1,0:T(8,128)(2,1)} %bitcast.3, bf16[768,3072]{1,0:T(8,128)(2,1)} %wo_hbm.1, ...), custom_call_target="tpu_custom_call" | custom-call | flops 19931332608 | bytes 22000000 | tf_op jit(solution)/shard_map/pallas_call | solution.py:525
  103.3 1.9 %copy.11 = bf16[1,384,768]{2,1,0:T(8,128)(2,1)} copy(bf16[1,384,768]{2,1,0:T(8,128)(2,1)} %get-tuple-element.6) | data formatting | bytes 1179648
  105.2 1.9 %copy.12 = bf16[1,384,768]{2,1,0:T(8,128)(2,1)} copy(bf16[1,384,768]{2,1,0:T(8,128)(2,1)} %get-tuple-element.7) | data formatting | bytes 1179648
  (1 shorter events, 0.0 us)

commit v2 on v1

--- a/solution.py
+++ b/solution.py
@@ -200,7 +200,7 @@
     has_right = z < size - 1
 
     load_lat = pltpu.make_async_copy(
-        lat_hbm.at[0], lat.at[z, h, pl.ds(0, tok)], load_sem.at[0]
+        lat_hbm.at[0], lat.at[z, h, pl.ds(EXTRA, tok)], load_sem.at[0]
     )
     load_modw = pltpu.make_async_copy(modw_hbm, modw, load_sem.at[1])
     load_w = pltpu.make_async_copy(w_hbm, w, load_sem.at[2])
@@ -222,71 +222,57 @@
         pl.semaphore_signal(barrier, inc=1, device_id={"pb": z + 1}, device_id_type=MESH)
 
     load_modw.wait()
-    gate_row = None
     lines = []
     for j in range(3):
         made = jnp.dot(emb_ref[...], modw[j], preferred_element_type=F32).astype(BF16)
         lines.append(made.astype(F32))
     gate[...] = lines[2][0:8]
     row_id = lax.broadcasted_iota(jnp.int32, (EXTRA, wid), 0)
-    lat[z, h, pl.ds(tok, EXTRA), :] = jnp.where(row_id == 0, lines[0], lines[1]).astype(BF16)
+    lat[z, h, pl.ds(0, EXTRA), :] = jnp.where(row_id == 0, lines[0], lines[1]).astype(BF16)
     load_lat.wait()
 
     waits = 2 + has_left.astype(jnp.int32) + has_right.astype(jnp.int32)
     pl.semaphore_wait(barrier, waits)
 
-    def to_left(f):
-        return pltpu.make_async_remote_copy(
-            lat.at[f, h], lat.at[f, h], left_sem.at[f], zr_sem.at[f], {"pb": z - 1}, MESH
-        )
-
-    def to_right(f):
-        return pltpu.make_async_remote_copy(
-            lat.at[f, h], lat.at[f, h], right_sem.at[f], zr_sem.at[f], {"pb": z + 1}, MESH
-        )
-
-    def to_x(f):
-        return pltpu.make_async_remote_copy(
-            lat.at[f, h], lat.at[f, h], xs_sem.at[f], xr_sem.at[f], {"ha": xp}, MESH
-        )
-
-    def from_x(f):
-        return pltpu.make_async_remote_copy(
-            lat.at[f, h], lat.at[f, xp], xs_sem.at[f], xr_sem.at[f], {"ha": xp}, MESH
-        )
-
-    def to_sib(f, which):
+    half = tok // 2
+    spans = (pl.ds(0, EXTRA + half), pl.ds(EXTRA + half, half))
+
+    def remote(f, m, quarter, send, recv, device):
+        ref = lat.at[f, quarter, spans[m]]
+        return pltpu.make_async_remote_copy(ref, ref, send.at[m, f], recv.at[m, f], device, MESH)
+
+    def to_left(f, m):
+        return remote(f, m, h, left_sem, zr_sem, {"pb": z - 1})
+
+    def to_right(f, m):
+        return remote(f, m, h, right_sem, zr_sem, {"pb": z + 1})
+
+    def to_x(f, m):
+        return remote(f, m, h, xs_sem, xr_sem, {"ha": xp})
+
+    def from_x(f, m):
+        return remote(f, m, xp, xs_sem, xr_sem, {"ha": xp})
+
+    def to_sib(f, m, which):
         quarter = h if which == 0 else xp
-        return pltpu.make_async_remote_copy(
-            lat.at[f, quarter],
-            lat.at[f, quarter],
-            ss_sem.at[which, f],
-            sr_sem.at[which, f],
-            {"ha": sib},
-            MESH,
-        )
-
-    def from_sib(f, which):
+        return remote(f, m, quarter, ss_sem.at[which], sr_sem.at[which], {"ha": sib})
+
+    def from_sib(f, m, which):
         quarter = sib if which == 0 else far
-        return pltpu.make_async_remote_copy(
-            lat.at[f, quarter],
-            lat.at[f, quarter],
-            ss_sem.at[which, f],
-            sr_sem.at[which, f],
-            {"ha": sib},
-            MESH,
-        )
-
-    @pl.when(has_left)
-    def _():
-        to_left(z).start()
-
-    @pl.when(has_right)
-    def _():
-        to_right(z).start()
-
-    to_x(z).start()
-    to_sib(z, 0).start()
+        return remote(f, m, quarter, ss_sem.at[which], sr_sem.at[which], {"ha": sib})
+
+    for m in range(2):
+
+        @pl.when(has_left)
+        def _():
+            to_left(z, m).start()
+
+        @pl.when(has_right)
+        def _():
+            to_right(z, m).start()
+
+        to_x(z, m).start()
+        to_sib(z, m, 0).start()
     load_w.start()
     load_wo.start()
 
@@ -297,52 +283,49 @@
     num[...] = jnp.zeros_like(num)
     den[...] = jnp.zeros_like(den)
 
-    orders = frame_order(size)
-    load_w.wait()
-
-    def step(s, carry):
-        d = s + 1
+    def forward(k):
+        d, m = k // 2 + 1, k % 2
 
         @pl.when(z + d < size)
         def _():
             f = z + d
-            to_right(f).wait_recv()
+            to_right(f, m).wait_recv()
 
             @pl.when(has_left)
             def _():
-                to_left(f).start()
-
-            to_x(f).start()
-            to_sib(f, 0).start()
+                to_left(f, m).start()
+
+            to_x(f, m).start()
+            to_sib(f, m, 0).start()
 
         @pl.when(z - d >= 0)
         def _():
             f = z - d
-            to_left(f).wait_recv()
+            to_left(f, m).wait_recv()
 
             @pl.when(has_right)
             def _():
-                to_right(f).start()
-
-            to_x(f).start()
-            to_sib(f, 0).start()
-
-        f = jnp.int32(0)
-        for i in range(size):
-            f = jnp.where(s == i, pick([o[i] for o in orders], z), f)
-        from_x(f).wait_recv()
-        to_sib(f, 1).start()
-        from_sib(f, 0).wait_recv()
-        from_sib(f, 1).wait_recv()
-
-        for q in range(4):
-            extra = lat[f, q, pl.ds(tok, EXTRA), :].astype(F32)
-            mods[0, :, q * wid : (q + 1) * wid] = jnp.broadcast_to(extra[0:1], (8, wid))
-            mods[1, :, q * wid : (q + 1) * wid] = jnp.broadcast_to(1.0 + extra[1:2], (8, wid))
+                to_right(f, m).start()
+
+            to_x(f, m).start()
+            to_sib(f, m, 0).start()
+
+    def norm_unit(f, m):
+        from_x(f, m).wait_recv()
+        to_sib(f, m, 1).start()
+        from_sib(f, m, 0).wait_recv()
+        from_sib(f, m, 1).wait_recv()
+        if m == 0:
+            for q in range(4):
+                cols = slice(q * wid, (q + 1) * wid)
+                extra = lat[f, q, pl.ds(0, EXTRA), :].astype(F32)
+                mods[0, :, cols] = jnp.broadcast_to(extra[0:1], (8, wid))
+                mods[1, :, cols] = jnp.broadcast_to(1.0 + extra[1:2], (8, wid))
 
         def norm_rows(t, inner):
-            r = pl.ds(pl.multiple_of(t * LN_ROWS, LN_ROWS), LN_ROWS)
-            parts = [lat[f, q, r, :].astype(F32) for q in range(4)]
+            r = pl.ds(pl.multiple_of(t * LN_ROWS + m * half, LN_ROWS), LN_ROWS)
+            src = pl.ds(pl.multiple_of(t * LN_ROWS + m * half + EXTRA, LN_ROWS), LN_ROWS)
+            parts = [lat[f, q, src, :].astype(F32) for q in range(4)]
             total = parts[0] + parts[1] + parts[2] + parts[3]
             mean = jnp.sum(total, axis=-1, keepdims=True) * (1.0 / full)
             parts = [part - mean for part in parts]
@@ -357,22 +340,26 @@
                 hid[r, cols] = out.astype(BF16)
             return inner
 
-        lax.fori_loop(0, tok // LN_ROWS, norm_rows, 0)
-
+        lax.fori_loop(0, half // LN_ROWS, norm_rows, 0, unroll=4)
+
+    def absorb_rows(rows, first):
         def one_pair(p, inner):
             cols = pl.ds(pl.multiple_of(p * 2 * HD, 2 * HD), 2 * HD)
-
-            @pl.when(s == 0)
-            def _():
+            if first:
+
+                @pl.when(p == 1)
+                def _():
+                    forward(2)
+
                 q2 = jnp.dot(hid[...], w[0, :, cols], preferred_element_type=F32)
                 halves = [
                     unit_rms(q2[:, i * HD : (i + 1) * HD]) / math.sqrt(HD) for i in range(2)
                 ]
                 qbuf[:, cols] = jnp.concatenate(halves, axis=1).astype(BF16)
 
-            k2 = jnp.dot(hid[...], w[1, :, cols], preferred_element_type=F32)
+            k2 = jnp.dot(hid[rows, :], w[1, :, cols], preferred_element_type=F32)
             keys = [unit_rms(k2[:, i * HD : (i + 1) * HD]).astype(BF16) for i in range(2)]
-            values = jnp.dot(hid[...], w[2, :, cols], preferred_element_type=F32).astype(BF16)
+            values = jnp.dot(hid[rows, :], w[2, :, cols], preferred_element_type=F32).astype(BF16)
             for i in range(2):
                 head = pl.ds(pl.multiple_of(p * 2 * HD + i * HD, HD), HD)
                 scores = lax.dot_general(
@@ -390,13 +377,48 @@
             return inner
 
         lax.fori_loop(0, pairs, one_pair, 0)
+
+    orders = frame_order(size)
+    forward(0)
+    norm_unit(z, 0)
+    forward(1)
+    norm_unit(z, 1)
+    load_w.wait()
+    absorb_rows(slice(0, tok), True)
+
+    def step(s, carry):
+        f = jnp.int32(0)
+        for i in range(1, size):
+            f = jnp.where(s == i, pick([o[i] for o in orders], z), f)
+        norm_unit(f, 0)
+
+        @pl.when(s == 1)
+        def _():
+            forward(3)
+
+        absorb_rows(slice(0, half), False)
+        norm_unit(f, 1)
+
+        @pl.when(s == 2)
+        def _():
+            forward(5)
+
+        absorb_rows(slice(half, tok), False)
+
+        @pl.when(s == 1)
+        def _():
+            forward(4)
+
         return carry
 
-    lax.fori_loop(0, size, step, 0)
+    lax.fori_loop(1, size, step, 0)
     load_wo.wait()
 
     def chunk(r):
         return pl.ds(pl.multiple_of(r * rows, rows), rows)
+
+    def token_rows(r):
+        return pl.ds(pl.multiple_of(r * rows + EXTRA, LN_ROWS), rows)
 
     def sib_copy(r):
         return pltpu.make_async_remote_copy(
@@ -452,7 +474,7 @@
     def finish(r, carry):
         x_copy(r).wait_recv()
         branch = own[r] + rbuf[r, 0].astype(F32) + xrecv[r].astype(F32)
-        latent = lat[z, h, chunk(r), :].astype(F32)
+        latent = lat[z, h, token_rows(r), :].astype(F32)
         adv[r] = (latent + gate[0:1] * branch).astype(BF16)
 
         @pl.when(has_left)
@@ -465,17 +487,18 @@
     lax.fori_loop(0, CHUNKS, finish, 0)
 
     def drain_frames(f, carry):
-        to_x(f).wait_send()
-        to_sib(f, 0).wait_send()
-        to_sib(f, 1).wait_send()
-
-        @pl.when(has_left & (f >= z))
-        def _():
-            to_left(f).wait_send()
-
-        @pl.when(has_right & (f <= z))
-        def _():
-            to_right(f).wait_send()
+        for m in range(2):
+            to_x(f, m).wait_send()
+            to_sib(f, m, 0).wait_send()
+            to_sib(f, m, 1).wait_send()
+
+            @pl.when(has_left & (f >= z))
+            def _():
+                to_left(f, m).wait_send()
+
+            @pl.when(has_right & (f <= z))
+            def _():
+                to_right(f, m).wait_send()
 
         return carry
 
@@ -511,6 +534,11 @@
     @pl.when(z == size - 1)
     def _():
         move_noise.wait()
+
+
+def land_kernel(a_ref, b_ref, a_out, b_out):
+    a_out[...] = a_ref[...]
+    b_out[...] = b_ref[...]
 
 
 def fused(size, latents, timesteps, mod_weight, qkv_weight, out_weight, noise_frame):
@@ -522,7 +550,7 @@
     anywhere = pl.BlockSpec(memory_space=pl.ANY)
     dma = pltpu.SemaphoreType.DMA
     flops = 2 * tok * full * wid * (1 + 2 * size) + 4 * tok * tok * size * wid + 2 * tok * wid * full
-    return pl.pallas_call(
+    outs = pl.pallas_call(
         functools.partial(block_kernel, size),
         out_shape=(
             jax.ShapeDtypeStruct(latents.shape, BF16),
@@ -550,13 +578,13 @@
             pltpu.VMEM((CHUNKS, rows, wid), BF16),
             pltpu.VMEM((CHUNKS, rows, wid), BF16),
             dma((5,)),
-            dma((size,)),
-            dma((size,)),
-            dma((size,)),
             dma((2, size)),
-            dma((size,)),
-            dma((size,)),
             dma((2, size)),
+            dma((2, size)),
+            dma((2, 2, size)),
+            dma((2, size)),
+            dma((2, size)),
+            dma((2, 2, size)),
             dma((CHUNKS,)),
             dma((CHUNKS,)),
             dma((CHUNKS,)),
@@ -580,6 +608,17 @@
         out_weight,
         noise_frame,
     )
+    piece = pl.BlockSpec((1, rows, wid), lambda i: (0, i, 0))
+    return pl.pallas_call(
+        land_kernel,
+        grid=(CHUNKS,),
+        out_shape=(
+            jax.ShapeDtypeStruct(latents.shape, BF16),
+            jax.ShapeDtypeStruct(latents.shape, BF16),
+        ),
+        in_specs=[piece, piece],
+        out_specs=(piece, piece),
+    )(*outs)
 
 
 def solution(mesh):

time: 108 us -> 101 us (0.935)
  local copies, waits for them, and re-layouts: 4.44 us -> 0.61 us
  Pallas kernels: 101 us -> 98.4 us
    pallas_call x1, Pallas kernels: 101 us -> 94.9 us  [fused(): pl.pallas_call(functools.partial(block_kernel, size), out_shape=(jax.Shap...]
    unnamed x2 -> x0, local copies, waits for them, and re-layouts: 3.83 us -> none
    pallas_call x0 -> x1, Pallas kernels: none -> 3.47 us  [fused(): pl.pallas_call(land_kernel, grid=(CHUNKS,), out_shape=(jax.ShapeDtypeStru...]
where the time goes in v2:
time: 101 us; the launch traced here: 100 us
  Pallas kernels  98.4 us (97%)
  between operations  1.3 us (1%)
    pallas_call x1, Pallas kernels, fused(): pl.pallas_call(functools.partial(block_kernel, size), out_shape=(jax.Shap...  94.9 us
    pallas_call x1, Pallas kernels, fused(): pl.pallas_call(land_kernel, grid=(CHUNKS,), out_shape=(jax.ShapeDtypeStru...  3.47 us

profile of v2, /device:TPU:0, one launch (start us, length us, event | category | flops | bytes accessed | tf_op | source)
XLA Modules:
  0.0 100.3 jit_solution(2120556067869074791)
XLA Ops:
  1.3 0.1 sine_convert_fusion
  1.3 0.6 broadcast_in_dim.2.emb_ref
  2.0 94.9 %shard_map.77 = (bf16[1,384,768]{2,1,0:T(8,128)(2,1)}, bf16[1,384,768]{2,1,0:T(8,128)(2,1)}) custom-call(bf16[16,256]{1,0:T(8,128)(2,1)} %broadcast_in_dim.2.emb_ref, bf16[1,384,768]{2,1,0:T(8,128)(2,1)} %lat_hbm.1, bf16[3,256,768]{2,1,0:T(8,128)(2,1)} %bitcast.4, bf16[3,3072,768]{2,1,0:T(8,128)(2,1)} %bitcast.3, bf16[768,3072]{1,0:T(8,128)(2,1)} %wo_hbm.1, ...), custom_call_target="tpu_custom_call" | custom-call | flops 19931332608 | bytes 22000000 | tf_op jit(solution)/shard_map/pallas_call | solution.py:553
  96.9 3.5 %shard_map.78 = (bf16[1,384,768]{2,1,0:T(8,128)(2,1)}, bf16[1,384,768]{2,1,0:T(8,128)(2,1)}) custom-call(bf16[1,384,768]{2,1,0:T(8,128)(2,1)} %get-tuple-element.4.a_ref, bf16[1,384,768]{2,1,0:T(8,128)(2,1)} %get-tuple-element.5.b_ref), custom_call_target="tpu_custom_call" | custom-call | tf_op jit(solution)/shard_map/pallas_call | solution.py:612
  (1 shorter events, 0.0 us)

commit v3 on v2

--- a/solution.py
+++ b/solution.py
@@ -399,15 +399,15 @@
         absorb_rows(slice(0, half), False)
         norm_unit(f, 1)
 
+        @pl.when(s == 1)
+        def _():
+            forward(4)
+
         @pl.when(s == 2)
         def _():
             forward(5)
 
         absorb_rows(slice(half, tok), False)
-
-        @pl.when(s == 1)
-        def _():
-            forward(4)
 
         return carry
 
@@ -608,10 +608,10 @@
         out_weight,
         noise_frame,
     )
-    piece = pl.BlockSpec((1, rows, wid), lambda i: (0, i, 0))
+    piece = pl.BlockSpec((1, tok, wid), lambda i: (0, 0, 0))
     return pl.pallas_call(
         land_kernel,
-        grid=(CHUNKS,),
+        grid=(1,),
         out_shape=(
             jax.ShapeDtypeStruct(latents.shape, BF16),
             jax.ShapeDtypeStruct(latents.shape, BF16),

time: 101 us -> 99.4 us (0.984)
  Pallas kernels: 98.4 us -> 97.2 us
    pallas_call x1, Pallas kernels: 3.47 us -> 2.29 us  [fused(): pl.pallas_call(land_kernel, grid=(1,), out_shape=(jax.ShapeDtypeStruct(la...]
where the time goes in v3:
time: 99.4 us; the launch traced here: 99.1 us
  Pallas kernels  97.2 us (98%)
  between operations  1.3 us (1%)
    pallas_call x1, Pallas kernels, fused(): pl.pallas_call(functools.partial(block_kernel, size), out_shape=(jax.Shap...  94.9 us
    pallas_call x1, Pallas kernels, fused(): pl.pallas_call(land_kernel, grid=(1,), out_shape=(jax.ShapeDtypeStruct(la...  2.29 us

profile of v3, /device:TPU:0, one launch (start us, length us, event | category | flops | bytes accessed | tf_op | source)
XLA Modules:
  0.0 99.1 jit_solution(9489478991500302159)
XLA Ops:
  1.3 0.1 sine_convert_fusion
  1.3 0.6 broadcast_in_dim.2.emb_ref
  2.0 94.9 %shard_map.77 = (bf16[1,384,768]{2,1,0:T(8,128)(2,1)}, bf16[1,384,768]{2,1,0:T(8,128)(2,1)}) custom-call(bf16[16,256]{1,0:T(8,128)(2,1)} %broadcast_in_dim.2.emb_ref, bf16[1,384,768]{2,1,0:T(8,128)(2,1)} %lat_hbm.1, bf16[3,256,768]{2,1,0:T(8,128)(2,1)} %bitcast.4, bf16[3,3072,768]{2,1,0:T(8,128)(2,1)} %bitcast.3, bf16[768,3072]{1,0:T(8,128)(2,1)} %wo_hbm.1, ...), custom_call_target="tpu_custom_call" | custom-call | flops 19931332608 | bytes 22000000 | tf_op jit(solution)/shard_map/pallas_call | solution.py:553
  96.8 2.3 %shard_map.78 = (bf16[1,384,768]{2,1,0:T(8,128)(2,1)}, bf16[1,384,768]{2,1,0:T(8,128)(2,1)}) custom-call(bf16[1,384,768]{2,1,0:T(8,128)(2,1)} %get-tuple-element.4.a_ref, bf16[1,384,768]{2,1,0:T(8,128)(2,1)} %get-tuple-element.5.b_ref), custom_call_target="tpu_custom_call" | custom-call | tf_op jit(solution)/shard_map/pallas_call | solution.py:612
  (1 shorter events, 0.0 us)
